TPU v7x, 1024 devices: a whole 4x8x16 slice. The times are simulated.
1024 devices in a mesh: row: 32 (over y, x_lo, core), col: 32 (over x_hi, z).
Axes of the slice: x: 4 (x_hi: 2, x_lo: 2; x = x_hi * 2 + x_lo), y: 8, z: 16, core: 2. Of those that a mesh axis runs over, the one named last changes fastest.
Arguments:
- iterate: bfloat16 [3584, 18432], P('row', 'col'), may hold values from -0.03125 to 0.03125
Outputs:
- update: float32 [3584, 18432], P('row', 'col')
All inputs are finite; a program needn't handle non-finite values.
Results may differ from a plain program's by a relative error of at most 0.0045.
Values may be sent and summed in bfloat16 or wider, within the bound.
No kernel may reach another device: no remote copies, remote signals or barrier semaphores. Data moves between devices by JAX's collectives and lax.ppermute only.
A program may use at most 32 MiB of HBM per device.

v0:
```python
import math

import jax
import jax.numpy as jnp
from jax import lax
from jax.sharding import PartitionSpec as P

M = 3584
N = 18432


def on_device(iterate):
    columns = lax.all_gather(iterate, "row", axis=0, tiled=True)
    total_rows = columns.shape[0]
    n_col = lax.axis_size("col")
    band_rows = total_rows // n_col
    gram_full = lax.psum(
        lax.dot_general(
            columns, iterate, (((1,), (1,)), ((), ())), preferred_element_type=jnp.float32
        ),
        "col",
    )
    gram_cols = gram_full.astype(jnp.bfloat16)
    local_block = lax.dynamic_slice_in_dim(
        gram_cols, lax.axis_index("col") * band_rows, band_rows, 0
    )
    gram_rows = lax.all_gather(local_block, "row", axis=1, tiled=True)
    square = jnp.dot(gram_rows, gram_cols, preferred_element_type=jnp.float32)
    polynomial = (-4.775 * local_block.astype(jnp.float32) + 2.0315 * square).astype(jnp.bfloat16)
    poly_cols = lax.all_gather(polynomial, "col", axis=0, tiled=True)
    product = lax.dot_general(
        poly_cols, columns, (((0,), (0,)), ((), ())), preferred_element_type=jnp.float32
    )
    scaling = 0.2 * math.sqrt(max(M, N))
    return scaling * (3.4445 * iterate.astype(jnp.float32) + product)


def solution(mesh):
    return jax.shard_map(
        on_device,
        mesh=mesh,
        in_specs=(P("row", "col"),),
        out_specs=P("row", "col"),
        check_vma=False,
    )
```

profile of v0, /device:TPU:64, one launch (start us, length us, event | category | flops | bytes accessed | tf_op | source)
XLA Modules:
  0.0 387.2 jit_solution(18104420451080772221)
XLA Ops:
  6.5 0.0 all-gather.2.cloned.1.call-start
  6.5 0.7 all-gather.2.cloned.1.call-update
  7.3 85.2 %all-gather.2.cloned.1.call-done = bf16[3584,576]{1,0:T(8,128)(2,1)} async-done(((bf16[112,576]{1,0:T(8,128)(2,1)}), bf16[3584,576]{1,0:T(8,128)(2,1)}) %all-gather.2.cloned.1.call-update) | async-done | bytes 4128784 | tf_op jit(solution)/shard_map/all_gather | solution.py:13
  92.4 3.8 fusion.3
  96.2 0.0 copy-start
  96.2 163.8 %all-reduce.1 = bf16[3584,112]{0,1:T(8,128)(2,1)S(1)} all-reduce(f32[3584,112]{0,1:T(8,128)S(1)} %fusion.3), channel_id=1, replica_groups=mesh['row'=32,'col'=32] {'col'}, use_global_device_ids=true, to_apply=%region_0.0 | all-reduce | flops 401408 | bytes 2408448 | tf_op jit(solution)/shard_map/psum | solution.py:17
  260.0 0.1 constant_dynamic-slice_fusion
  260.1 34.3 %all_gather.10 = bf16[112,3584]{0,1:T(8,128)(2,1)S(1)} all-gather(bf16[112,112]{0,1:T(8,128)(2,1)S(1)} %constant_dynamic-slice_fusion), channel_id=1, replica_groups=mesh['row'=32,'col'=32] {'row'}, dimensions={1}, use_global_device_ids=true | all-gather | bytes 827904 | tf_op jit(solution)/shard_map/all_gather | solution.py:27
  294.4 0.4 fusion.2
  294.8 0.1 copy.2
  294.9 81.5 %all_gather.11 = bf16[3584,112]{1,0:T(8,128)(2,1)S(1)} all-gather(bf16[112,112]{1,0:T(8,128)(2,1)S(1)} %copy.2), channel_id=1, replica_groups=mesh['row'=32,'col'=32] {'col'}, dimensions={0}, use_global_device_ids=true | all-gather | bytes 827904 | tf_op jit(solution)/shard_map/all_gather | solution.py:30
  376.4 0.0 copy-done
  376.4 3.9 %fusion = f32[112,576]{1,0:T(8,128)} fusion(bf16[3584,112]{1,0:T(8,128)(2,1)S(1)} %all_gather.11, bf16[3584,576]{1,0:T(8,128)(2,1)} %all-gather.2.cloned.1.call-done, bf16[112,576]{1,0:T(8,128)(2,1)S(1)} %copy-done), kind=kOutput, calls=%fused_computation.1 | convolution fusion | flops 462680064 | bytes 5318656 | tf_op jit(solution)/shard_map/dot_general | solution.py:31
Async XLA Ops:
  6.5 85.9 %all-gather.2.cloned.1.call-start = ((), (), s32[]{:S(2)}) async-start(), calls=%async_computation | async-start | bytes 4730880 | tf_op jit(solution)/shard_map/all_gather | solution.py:13
  96.2 280.2 %copy-start = (bf16[112,576]{1,0:T(8,128)(2,1)S(1)}, bf16[112,576]{1,0:T(8,128)(2,1)}, u32[]{:S(2)}) copy-start(bf16[112,576]{1,0:T(8,128)(2,1)} %param.1) | copy-start | bytes 387076
Sparse Core Ops, SparseCore 0:
  10.1 82.2 all-gather.1
where the time goes:
time: 387 us
  blocking collectives  280 us (72%)
  waiting for transfers between devices  85.9 us (22%)
  between operations  13.4 us (3%)
  matrix products  8.11 us (2%)
    psum x1, blocking collectives, on_device(): lax.psum(lax.dot_general(columns, iterate, (((1,), (1,)), ((), ())), pref...  164 us
    all_gather x1, waiting for transfers between devices, on_device(): columns = lax.all_gather(iterate, 'row', axis=0, tiled=True)  85.2 us
    all_gather x1, blocking collectives, on_device(): poly_cols = lax.all_gather(polynomial, 'col', axis=0, tiled=True)  81.5 us
    all_gather x1, blocking collectives, on_device(): gram_rows = lax.all_gather(local_block, 'row', axis=1, tiled=True)  34.3 us
  transfers between devices with their start and end apart: 1, of which 1 were waited for; matrix products, arithmetic and copies ran while one was open for 0% of the time, Pallas kernels for 0%

commit v1 on v0

v1 whole, which is shorter than its diff:
```python
import math

import jax
import jax.numpy as jnp
from jax import lax
from jax.sharding import Mesh
from jax.sharding import PartitionSpec as P

M = 3584
N = 18432
BLOCK = 112
HALF = 56
SWAP = [(0, 1), (1, 0)]


def f32(value):
    return value.astype(jnp.float32)


def bf16(value):
    return value.astype(jnp.bfloat16)


def dot(a, b, dims):
    return lax.dot_general(a, b, ((dims[0:1], dims[1:2]), ((), ())), preferred_element_type=jnp.float32)


def swap(value, axis):
    return lax.ppermute(value, axis, SWAP)


def gather_panel(block):
    own = lax.all_gather(block, "y", axis=0)
    return own, swap(own, "c")


def apply_gram(gram, own, other):
    width = own.shape[-1]
    near, far = gram[: 8 * BLOCK], gram[8 * BLOCK :]
    part = dot(near, own.reshape(8 * BLOCK, width), (0, 0))
    part = part + dot(far, other.reshape(8 * BLOCK, width), (0, 0))
    part = part.reshape(2, BLOCK, width)
    return part[0] + f32(swap(bf16(part[1]), "l"))


def on_device(iterate):
    h = lax.axis_index("h")
    band = jnp.concatenate([iterate, swap(iterate, "l")], axis=0)
    own, other = gather_panel(iterate)
    width = iterate.shape[-1]

    def gram_half(which):
        parts = []
        for panel in (own, other):
            rows = lax.dynamic_slice_in_dim(panel, which * HALF, HALF, 1)
            parts.append(dot(rows.reshape(8 * HALF, width), band, (1, 1)))
        return jnp.concatenate(parts, axis=0)

    received = swap(bf16(gram_half(1 - h)), "h")
    pieces = bf16(gram_half(h) + f32(received)).reshape(16, HALF, 2 * BLOCK)
    pieces = lax.all_to_all(pieces, "z", 0, 0, tiled=True)
    gram = bf16(f32(pieces).sum(0))
    gram = lax.all_gather(gram, "h", axis=0)
    gram = lax.all_gather(gram, "z", axis=0)
    gram = gram.reshape(16 * BLOCK, 2 * BLOCK)

    first = apply_gram(gram, own, other)
    second = apply_gram(gram, *gather_panel(bf16(first)))
    scaling = 0.2 * math.sqrt(max(M, N))
    return scaling * (3.4445 * f32(iterate) - 4.775 * first + 2.0315 * second)


def solution(mesh):
    grid = Mesh(mesh.devices.reshape(8, 2, 2, 2, 16), ("y", "l", "c", "h", "z"))
    spec = P(("y", "l", "c"), ("h", "z"))
    return jax.shard_map(
        on_device, mesh=grid, in_specs=(spec,), out_specs=spec, check_vma=False
    )
```

time: 387 us -> 190 us (0.49)
  the two profiles are of different devices: /device:TPU:64 before, /device:TPU:1 now
where the time goes in v1:
time: 190 us; the launch traced here: 189 us
  blocking collectives  109 us (57%)
  starting transfers between devices  49.5 us (26%)
  waiting for transfers between devices  25.2 us (13%)
  matrix products  3.68 us (2%)
    ppermute x6, starting transfers between devices, swap(): return lax.ppermute(value, axis, SWAP)  49.5 us
    all_gather x2, blocking collectives, gather_panel(): own = lax.all_gather(block, 'y', axis=0)  44.7 us
    all_gather x1, blocking collectives, on_device(): gram = lax.all_gather(gram, 'z', axis=0)  32.1 us
    all_to_all x1, blocking collectives, on_device(): pieces = lax.all_to_all(pieces, 'z', 0, 0, tiled=True)  27 us
    ppermute x6, waiting for transfers between devices, swap(): return lax.ppermute(value, axis, SWAP)  25.2 us
    all_gather x1, blocking collectives, on_device(): gram = lax.all_gather(gram, 'h', axis=0)  5.2 us
  transfers between devices with their start and end apart: 6, of which 5 were waited for; matrix products, arithmetic and copies ran while one was open for 1% of the time, Pallas kernels for 0%

profile of v1, /device:TPU:1, one launch (start us, length us, event | category | flops | bytes accessed | tf_op | source)
XLA Modules:
  0.0 189.3 jit_solution(9798484989374037108)
XLA Ops:
  0.0 23.5 %all-gather = bf16[896,576]{1,0:T(8,128)(2,1)S(1)} all-gather(bf16[112,576]{1,0:T(8,128)(2,1)} %param.1), channel_id=2, replica_groups=mesh['y'=8,'l'=2,'c'=2,'h'=2,'z'=16] {'y'}, dimensions={0}, use_global_device_ids=true | all-gather | bytes 1161216 | tf_op jit(solution)/shard_map/all_gather | solution.py:33
  23.5 20.0 %collective-permute-start.1 = (bf16[8,112,576]{2,1,0:T(8,128)(2,1)S(1)}, bf16[8,112,576]{2,1,0:T(8,128)(2,1)S(1)}, u32[]{:S(2)}, u32[]{:S(2)}) collective-permute-start(bf16[8,112,576]{2,1,0:T(8,128)(2,1)S(1)} %bitcast.28), channel_id=1, source_target_pairs={{0,32},{32,0},{1,33},{33,1},{2,34},{34,2},{3,35},{35,3},{4,36},{36... | collective-permute-start | bytes 3096584 | tf_op jit(solution)/shard_map/ppermute | solution.py:29
  43.4 1.9 %collective-permute-start = (bf16[112,576]{1,0:T(8,128)(2,1)S(1)}, bf16[112,576]{1,0:T(8,128)(2,1)S(1)}, u32[]{:S(2)}, u32[]{:S(2)}) collective-permute-start(bf16[112,576]{1,0:T(8,128)(2,1)S(1)} %copy-done), channel_id=1, source_target_pairs={{0,64},{64,0},{1,65},{65,1},{2,66},{66,2},{3,67},{67,3},{4,68},{68... | collective-permute-start | bytes 387080 | tf_op jit(solution)/shard_map/ppermute | solution.py:29
  45.4 0.2 constant_dynamic-slice_fusion.1
  45.6 5.2 %collective-permute-done = bf16[112,576]{1,0:T(8,128)(2,1)S(1)} collective-permute-done((bf16[112,576]{1,0:T(8,128)(2,1)S(1)}, bf16[112,576]{1,0:T(8,128)(2,1)S(1)}, u32[]{:S(2)}, u32[]{:S(2)}) %collective-permute-start) | collective-permute-done | bytes 129056 | tf_op jit(solution)/shard_map/ppermute | solution.py:29
  50.7 0.4 convolution_convert_fusion.1
  51.1 0.2 constant_dynamic-slice_fusion
  51.3 0.4 convolution_convert_fusion
  51.7 0.1 pad_maximum_fusion
  51.8 1.9 %collective-permute-start.2 = (bf16[896,224]{0,1:T(8,128)(2,1)S(1)}, bf16[896,224]{0,1:T(8,128)(2,1)S(1)}, u32[]{:S(2)}, u32[]{:S(2)}) collective-permute-start(bf16[896,224]{0,1:T(8,128)(2,1)S(1)} %pad_maximum_fusion), channel_id=1, source_target_pairs={{0,16},{16,0},{1,17},{17,1},{2,18},{18,2},{3,19},{19,3},{4,20},{20... | collective-permute-start | bytes 1204232 | tf_op jit(solution)/shard_map/ppermute | solution.py:29
  53.7 0.4 fusion.6
  54.1 0.4 fusion.7
  54.5 10.7 %collective-permute-done.2 = bf16[896,224]{0,1:T(8,128)(2,1)S(1)} collective-permute-done((bf16[896,224]{0,1:T(8,128)(2,1)S(1)}, bf16[896,224]{0,1:T(8,128)(2,1)S(1)}, u32[]{:S(2)}, u32[]{:S(2)}) %collective-permute-start.2) | collective-permute-done | bytes 401440 | tf_op jit(solution)/shard_map/ppermute | solution.py:29
  65.2 0.2 fusion
  65.4 0.2 copy.3
  65.6 27.0 %all_to_all.5 = bf16[16,56,224]{2,1,0:T(8,128)(2,1)S(1)} all-to-all(bf16[16,56,224]{2,1,0:T(8,128)(2,1)S(1)} %bitcast.40), channel_id=1, replica_groups=mesh['y'=8,'l'=2,'c'=2,'h'=2,'z'=16] {'z'}, dimensions={0} | all-to-all | bytes 802816 | tf_op jit(solution)/shard_map/all_to_all | solution.py:61
  92.6 0.1 reduce_sum.12
  92.7 5.2 %all-gather.1 = bf16[112,224]{1,0:T(8,128)(2,1)S(1)} all-gather(bf16[56,224]{1,0:T(8,128)(2,1)S(1)} %reduce_sum.12), channel_id=3, replica_groups=mesh['y'=8,'l'=2,'c'=2,'h'=2,'z'=16] {'h'}, dimensions={0}, use_global_device_ids=true | all-gather | bytes 75264 | tf_op jit(solution)/shard_map/all_gather | solution.py:63
  97.9 32.1 %all-gather.2 = bf16[32,56,224]{2,1,0:T(8,128)(2,1)S(1)} all-gather(bf16[2,56,224]{2,1,0:T(8,128)(2,1)S(1)} %bitcast.42), channel_id=4, replica_groups=mesh['y'=8,'l'=2,'c'=2,'h'=2,'z'=16] {'z'}, dimensions={0}, use_global_device_ids=true | all-gather | bytes 852992 | tf_op jit(solution)/shard_map/all_gather | solution.py:64
  130.0 0.1 fusion.5
  130.0 0.5 fusion.8
  130.6 0.5 convolution_add_fusion.1
  131.2 3.1 %collective-permute-start.3 = (bf16[112,576]{1,0:T(8,128)(2,1)S(1)}, bf16[112,576]{1,0:T(8,128)(2,1)S(1)}, u32[]{:S(2)}, u32[]{:S(2)}) collective-permute-start(bf16[112,576]{1,0:T(8,128)(2,1)S(1)} %slice.63), channel_id=1, source_target_pairs={{0,64},{64,0},{1,65},{65,1},{2,66},{66,2},{3,67},{67,3},{4,68},{68... | collective-permute-start | bytes 387080 | tf_op jit(solution)/shard_map/ppermute | solution.py:29
  134.3 2.7 %collective-permute-done.3 = bf16[112,576]{1,0:T(8,128)(2,1)S(1)} collective-permute-done((bf16[112,576]{1,0:T(8,128)(2,1)S(1)}, bf16[112,576]{1,0:T(8,128)(2,1)S(1)}, u32[]{:S(2)}, u32[]{:S(2)}) %collective-permute-start.3) | collective-permute-done | bytes 129056 | tf_op jit(solution)/shard_map/ppermute | solution.py:29
  137.1 21.2 %all-gather.3 = bf16[896,576]{1,0:T(8,128)(2,1)S(1)} all-gather(bf16[112,576]{1,0:T(8,128)(2,1)S(1)} %fusion.4), channel_id=5, replica_groups=mesh['y'=8,'l'=2,'c'=2,'h'=2,'z'=16] {'y'}, dimensions={0}, use_global_device_ids=true | all-gather | bytes 1161216 | tf_op jit(solution)/shard_map/all_gather | solution.py:33
  158.3 19.8 %collective-permute-start.4 = (bf16[8,112,576]{2,1,0:T(8,128)(2,1)S(1)}, bf16[8,112,576]{2,1,0:T(8,128)(2,1)S(1)}, u32[]{:S(2)}, u32[]{:S(2)}) collective-permute-start(bf16[8,112,576]{2,1,0:T(8,128)(2,1)S(1)} %bitcast.30), channel_id=1, source_target_pairs={{0,32},{32,0},{1,33},{33,1},{2,34},{34,2},{3,35},{35,3},{4,36},{36... | collective-permute-start | bytes 3096584 | tf_op jit(solution)/shard_map/ppermute | solution.py:29
  178.1 2.4 %collective-permute-done.4 = bf16[8,112,576]{2,1,0:T(8,128)(2,1)S(1)} collective-permute-done((bf16[8,112,576]{2,1,0:T(8,128)(2,1)S(1)}, bf16[8,112,576]{2,1,0:T(8,128)(2,1)S(1)}, u32[]{:S(2)}, u32[]{:S(2)}) %collective-permute-start.4) | collective-permute-done | bytes 1032224 | tf_op jit(solution)/shard_map/ppermute | solution.py:29
  180.5 0.5 fusion.9
  181.1 0.5 convolution_add_fusion
  181.6 2.7 %collective-permute-start.5 = (bf16[112,576]{1,0:T(8,128)(2,1)S(1)}, bf16[112,576]{1,0:T(8,128)(2,1)S(1)}, u32[]{:S(2)}, u32[]{:S(2)}) collective-permute-start(bf16[112,576]{1,0:T(8,128)(2,1)S(1)} %slice.62), channel_id=1, source_target_pairs={{0,64},{64,0},{1,65},{65,1},{2,66},{66,2},{3,67},{67,3},{4,68},{68... | collective-permute-start | bytes 387080 | tf_op jit(solution)/shard_map/ppermute | solution.py:29
  184.4 4.1 %collective-permute-done.5 = bf16[112,576]{1,0:T(8,128)(2,1)S(1)} collective-permute-done((bf16[112,576]{1,0:T(8,128)(2,1)S(1)}, bf16[112,576]{1,0:T(8,128)(2,1)S(1)}, u32[]{:S(2)}, u32[]{:S(2)}) %collective-permute-start.5) | collective-permute-done | bytes 129056 | tf_op jit(solution)/shard_map/ppermute | solution.py:29
  188.5 0.8 fusion.3
  (8 shorter events, 0.1 us)
Async XLA Ops:
  0.0 43.4 %copy-start = (bf16[112,576]{1,0:T(8,128)(2,1)S(1)}, bf16[112,576]{1,0:T(8,128)(2,1)}, u32[]{:S(2)}) copy-start(bf16[112,576]{1,0:T(8,128)(2,1)} %param.1) | copy-start | bytes 387076
  23.5 27.7 %collective-permute-start.1 = (bf16[8,112,576]{2,1,0:T(8,128)(2,1)S(1)}, bf16[8,112,576]{2,1,0:T(8,128)(2,1)S(1)}, u32[]{:S(2)}, u32[]{:S(2)}) collective-permute-start(bf16[8,112,576]{2,1,0:T(8,128)(2,1)S(1)} %bitcast.28), channel_id=1, source_target_pairs={{0,32},{32,0},{1,33},{33,1},{2,34},{34,2},{3,35},{35,3},{4,36},{36... | collective-permute-start | bytes 3096584 | tf_op jit(solution)/shard_map/ppermute | solution.py:29
  43.4 7.3 %collective-permute-start = (bf16[112,576]{1,0:T(8,128)(2,1)S(1)}, bf16[112,576]{1,0:T(8,128)(2,1)S(1)}, u32[]{:S(2)}, u32[]{:S(2)}) collective-permute-start(bf16[112,576]{1,0:T(8,128)(2,1)S(1)} %copy-done), channel_id=1, source_target_pairs={{0,64},{64,0},{1,65},{65,1},{2,66},{66,2},{3,67},{67,3},{4,68},{68... | collective-permute-start | bytes 387080 | tf_op jit(solution)/shard_map/ppermute | solution.py:29
  51.8 13.4 %collective-permute-start.2 = (bf16[896,224]{0,1:T(8,128)(2,1)S(1)}, bf16[896,224]{0,1:T(8,128)(2,1)S(1)}, u32[]{:S(2)}, u32[]{:S(2)}) collective-permute-start(bf16[896,224]{0,1:T(8,128)(2,1)S(1)} %pad_maximum_fusion), channel_id=1, source_target_pairs={{0,16},{16,0},{1,17},{17,1},{2,18},{18,2},{3,19},{19,3},{4,20},{20... | collective-permute-start | bytes 1204232 | tf_op jit(solution)/shard_map/ppermute | solution.py:29
  131.2 5.8 %collective-permute-start.3 = (bf16[112,576]{1,0:T(8,128)(2,1)S(1)}, bf16[112,576]{1,0:T(8,128)(2,1)S(1)}, u32[]{:S(2)}, u32[]{:S(2)}) collective-permute-start(bf16[112,576]{1,0:T(8,128)(2,1)S(1)} %slice.63), channel_id=1, source_target_pairs={{0,64},{64,0},{1,65},{65,1},{2,66},{66,2},{3,67},{67,3},{4,68},{68... | collective-permute-start | bytes 387080 | tf_op jit(solution)/shard_map/ppermute | solution.py:29
  158.3 22.2 %collective-permute-start.4 = (bf16[8,112,576]{2,1,0:T(8,128)(2,1)S(1)}, bf16[8,112,576]{2,1,0:T(8,128)(2,1)S(1)}, u32[]{:S(2)}, u32[]{:S(2)}) collective-permute-start(bf16[8,112,576]{2,1,0:T(8,128)(2,1)S(1)} %bitcast.30), channel_id=1, source_target_pairs={{0,32},{32,0},{1,33},{33,1},{2,34},{34,2},{3,35},{35,3},{4,36},{36... | collective-permute-start | bytes 3096584 | tf_op jit(solution)/shard_map/ppermute | solution.py:29
  181.6 6.9 %collective-permute-start.5 = (bf16[112,576]{1,0:T(8,128)(2,1)S(1)}, bf16[112,576]{1,0:T(8,128)(2,1)S(1)}, u32[]{:S(2)}, u32[]{:S(2)}) collective-permute-start(bf16[112,576]{1,0:T(8,128)(2,1)S(1)} %slice.62), channel_id=1, source_target_pairs={{0,64},{64,0},{1,65},{65,1},{2,66},{66,2},{3,67},{67,3},{4,68},{68... | collective-permute-start | bytes 387080 | tf_op jit(solution)/shard_map/ppermute | solution.py:29
